TPU v7x, 256 devices: a whole 4x4x8 slice. The times are simulated.
256 devices in a mesh: rows: 64 (over x, y_lo, z), cols: 4 (over y_hi, core).
Axes of the slice: x: 4, y: 4 (y_hi: 2, y_lo: 2; y = y_hi * 2 + y_lo), z: 8, core: 2. Of those that a mesh axis runs over, the one named last changes fastest.
Arguments:
- right_side: float32 [32, 131072], P(None, ('rows', 'cols')), may hold values from -6 to 6
- local_inverse: float32 [64, 4, 1024, 1024], P('rows', 'cols'), may hold values from -1 to 2.5, as said below
- modes: float32 [64, 4, 64, 1024], P('rows', 'cols'), may hold values from -0.1875 to 0.1875
- coarse_inverse: float32 [16384, 16384], P('rows', 'cols'), may hold values from -1 to 2.5, as said below
- stiff_diag: float32 [64, 4, 1024], P('rows', 'cols'), may hold values from 1 to 4
- nbr_index: int32 [64, 4, 80, 1024], P('rows', 'cols'), may hold values from 0 to 1023
- nbr_coef: float32 [64, 4, 80, 1024], P('rows', 'cols'), may hold values from -0.625 to 0.625
- send_rows: int32 [64, 4, 4, 128], P('rows', 'cols'), may hold values from 0 to 511
Outputs:
- solution: float32 [32, 131072], P(None, ('rows', 'cols'))
- residual: float32 [32, 131072], P(None, ('rows', 'cols'))
Inputs may be any that keep to these rules, and one draw needn't show every extreme that they name: `local_inverse`: each subdomain inverse has a diagonal between 0.25 and 2 and small off-diagonal entries. `coarse_inverse`: a diagonal between 0.25 and 2 at entries whose row and column name the same coarse unknown, small entries elsewhere.
All inputs are finite; a program needn't handle non-finite values.
Results may differ from a plain program's by a relative error of at most 0.00013.
Values sent between devices are 32-bit elements; how exact they have to be, the bound alone decides.
A program may use at most 128 MiB of HBM per device.

v0:
```python
import jax
import jax.numpy as jnp
from jax import lax
from jax.sharding import PartitionSpec as P


def from_behind(block, axis, distance):
    devices = range(lax.axis_size(axis))
    route = [(i - distance, i) for i in devices if i - distance in devices]
    return lax.ppermute(block, axis, route)


def along_rows(block, offset):
    return from_behind(block, "rows", offset)


def along_cols(block, offset):
    return from_behind(block, "cols", offset)


def extend(owned, sends):
    picked = [owned[:, sends[e]] for e in range(4)]
    first = along_rows(picked[0], 1)
    second = along_rows(picked[1], -1)
    third = along_cols(picked[2], 1)
    fourth = along_cols(picked[3], -1)
    return jnp.concatenate([owned, first, second, third, fourth], axis=1)


def fold(sub, sends, own_count, block_rows):
    owned = sub[:, :own_count]
    bands = [
        sub[:, own_count + e * block_rows : own_count + (e + 1) * block_rows] for e in range(4)
    ]
    backs = [
        along_rows(bands[0], -1),
        along_rows(bands[1], 1),
        along_cols(bands[2], -1),
        along_cols(bands[3], 1),
    ]
    for e in range(4):
        owned = owned.at[:, sends[e]].add(backs[e])
    return owned


def coarse_apply(restricted, coarse_block):
    highest = lax.Precision.HIGHEST
    partial_sum = lax.dot_general(
        lax.all_gather(restricted, "rows", axis=1, tiled=True),
        coarse_block,
        (((1,), (1,)), ((), ())),
        precision=highest,
        preferred_element_type=jnp.float32,
    )
    return lax.psum_scatter(partial_sum, "cols", scatter_dimension=1, tiled=True)


def couple(sub, diag, index, coef):
    coupled = diag[None, :] * sub
    count = index.shape[0]
    group = min(16, count)
    for begin in range(0, count, group):
        finish = min(begin + group, count)
        nearby = sub[:, index[begin:finish]]
        coupled = coupled + jnp.sum(nearby * coef[None, begin:finish, :], axis=1)
    return coupled


def body(
    right_side, local_inverse, modes, coarse_inverse, stiff_diag, nbr_index, nbr_coef, send_rows
):
    highest = lax.Precision.HIGHEST
    inverse = local_inverse[0, 0]
    basis = modes[0, 0]
    diag = stiff_diag[0, 0]
    index = nbr_index[0, 0]
    coef = nbr_coef[0, 0]
    sends = send_rows[0, 0]
    own_count = right_side.shape[1]
    block_rows = sends.shape[1]

    def precondition(resid):
        sub = extend(resid, sends)
        local = lax.dot_general(
            sub,
            inverse,
            (((1,), (1,)), ((), ())),
            precision=highest,
            preferred_element_type=jnp.float32,
        )
        restricted = lax.dot_general(
            sub,
            basis,
            (((1,), (1,)), ((), ())),
            precision=highest,
            preferred_element_type=jnp.float32,
        )
        coarse = coarse_apply(restricted, coarse_inverse)
        local = local + jnp.dot(
            coarse, basis, precision=highest, preferred_element_type=jnp.float32
        )
        return fold(local, sends, own_count, block_rows)

    first = precondition(right_side)
    sub = extend(first, sends)
    coupled = couple(sub, diag, index, coef)
    image = fold(coupled, sends, own_count, block_rows)
    residual = right_side - image
    solution = first + precondition(residual)
    return (solution, residual)


def solution(mesh):
    in_specs = (
        P(None, ("rows", "cols")),
        P("rows", "cols", None, None),
        P("rows", "cols", None, None),
        P("rows", "cols"),
        P("rows", "cols", None),
        P("rows", "cols", None, None),
        P("rows", "cols", None, None),
        P("rows", "cols", None, None),
    )
    out_specs = (P(None, ("rows", "cols")), P(None, ("rows", "cols")))
    return jax.shard_map(body, mesh=mesh, in_specs=in_specs, out_specs=out_specs, check_vma=False)
```

profile of v0, /device:TPU:120, one launch (start us, length us, event | category | flops | bytes accessed | tf_op | source)
XLA Modules:
  0.0 825.7 jit_solution(2240018692300086383)
XLA Ops:
  9.7 5.0 collective-permute-start
  15.4 1.9 collective-permute-start.1
  18.0 1.9 collective-permute-start.2
  20.5 5.1 collective-permute-start.3
  28.4 136.5 %all-gather = f32[64,64,32]{1,2,0:T(8,128)S(1)} all-gather(f32[1,64,32]{1,2,0:T(8,128)S(1)} %convolution_bitcast_fusion.3), channel_id=1, replica_groups=mesh['rows'=64,'cols'=4] {'rows'}, dimensions={0}, use_global_device_ids=true | all-gather | bytes 532480 | tf_op jit(solution)/shard_map/all_gather | solution.py:49
  165.9 5.8 convolution_bitcast_fusion.1
  171.7 49.3 %reduce-scatter.7.cloned.1.call-done = f32[64,32]{1,0:T(8,128)} async-done(((f32[256,32]{1,0:T(8,128)}), f32[64,32]{1,0:T(8,128)}) %reduce-scatter.7.cloned.1.call-update) | async-done | bytes 8208
  222.1 6.0 fusion.4
  228.2 1.9 collective-permute-start.7
  230.1 5.1 collective-permute-start.6
  235.2 4.7 collective-permute-start.5
  239.9 1.9 collective-permute-start.4
  242.0 4.7 collective-permute-done.4
  253.3 1.9 collective-permute-start.8
  257.2 3.9 collective-permute-start.9
  261.1 1.9 collective-permute-start.10
  263.1 5.3 collective-permute-start.11
  268.5 1.6 collective-permute-done.11
  270.1 54.4 %gather_fusion.12 = f32[16384,32]{1,0:T(8,128)} fusion(f32[32,1024]{0,1:T(8,128)S(1)} %constant_dynamic-update-slice_fusion.5, s32[16384]{0:T(1024)S(1)} %broadcast_clamp_fusion), kind=kCustom, calls=%fused_computation.12 | custom fusion | bytes 4259840 | tf_op jit(solution)/shard_map/gather | solution.py:64
  324.5 54.4 %gather_fusion.11 = f32[16384,32]{1,0:T(8,128)} fusion(f32[32,1024]{0,1:T(8,128)S(1)} %constant_dynamic-update-slice_fusion.5, s32[16384]{0:T(1024)S(1)} %broadcast_clamp_fusion.1), kind=kCustom, calls=%fused_computation.11 | custom fusion | bytes 4259840 | tf_op jit(solution)/shard_map/gather | solution.py:64
  378.9 54.4 %gather_fusion.10 = f32[16384,32]{1,0:T(8,128)} fusion(f32[32,1024]{0,1:T(8,128)S(1)} %constant_dynamic-update-slice_fusion.5, s32[16384]{0:T(1024)S(1)} %broadcast_clamp_fusion.2), kind=kCustom, calls=%fused_computation.10 | custom fusion | bytes 4259840 | tf_op jit(solution)/shard_map/gather | solution.py:64
  433.3 54.4 %gather_fusion.9 = f32[16384,32]{1,0:T(8,128)} fusion(f32[32,1024]{0,1:T(8,128)S(1)} %constant_dynamic-update-slice_fusion.5, s32[16384]{0:T(1024)S(1)} %broadcast_clamp_fusion.3), kind=kCustom, calls=%fused_computation.9 | custom fusion | bytes 4259840 | tf_op jit(solution)/shard_map/gather | solution.py:64
  487.7 54.3 %gather_fusion.8 = f32[16384,32]{1,0:T(8,128)} fusion(f32[32,1024]{0,1:T(8,128)S(1)} %constant_dynamic-update-slice_fusion.5, s32[16384]{0:T(1024)S(1)} %broadcast_clamp_fusion.4), kind=kCustom, calls=%fused_computation.8 | custom fusion | bytes 4259840 | tf_op jit(solution)/shard_map/gather | solution.py:64
  542.0 5.6 multiply_reduce_fusion
  547.6 5.4 multiply_reduce_fusion.1
  553.1 2.5 multiply_reduce_fusion.2
  555.7 2.5 multiply_reduce_fusion.3
  558.2 2.5 multiply_reduce_fusion.4
  561.0 1.9 collective-permute-start.12
  562.9 5.1 collective-permute-start.13
  568.0 4.6 collective-permute-start.14
  572.7 1.9 collective-permute-start.15
  574.6 1.4 scatter_custom_fusion.4
  577.4 1.4 scatter_custom_fusion.6
  583.9 2.2 collective-permute-start.16
  586.1 3.6 collective-permute-start.17
  589.7 1.9 collective-permute-start.18
  591.6 5.1 collective-permute-start.19
  597.0 1.6 collective-permute-done.19
  599.1 132.8 %all-gather.1 = f32[64,64,32]{1,2,0:T(8,128)S(1)} all-gather(f32[1,64,32]{1,2,0:T(8,128)S(1)} %convolution_bitcast_fusion.2), channel_id=1, replica_groups=mesh['rows'=64,'cols'=4] {'rows'}, dimensions={0}, use_global_device_ids=true | all-gather | bytes 532480 | tf_op jit(solution)/shard_map/all_gather | solution.py:49
  732.9 5.8 convolution_bitcast_fusion
  738.8 47.6 %reduce-scatter.9.cloned.1.call-done = f32[64,32]{1,0:T(8,128)} async-done(((f32[256,32]{1,0:T(8,128)}), f32[64,32]{1,0:T(8,128)}) %reduce-scatter.9.cloned.1.call-update) | async-done | bytes 8208
  787.5 6.0 fusion.7
  793.6 1.9 collective-permute-start.23
  795.5 5.1 collective-permute-start.22
  800.6 4.7 collective-permute-start.21
  805.3 1.9 collective-permute-start.20
  807.4 4.8 collective-permute-done.20
  (134 shorter events, 34.0 us)
Async XLA Ops:
  7.2 20.9 %copy-start = (f32[1,1,64,1024]{3,2,1,0:T(8,128)S(1)}, f32[1,1,64,1024]{3,2,1,0:T(8,128)}, u32[]{:S(2)}) copy-start(f32[1,1,64,1024]{3,2,1,0:T(8,128)} %param.10) | copy-start | bytes 786436
  7.2 213.9 %reduce-scatter.7.cloned.1.call-start = ((), (), s32[]{:S(2)}) async-start(), calls=%async_computation.2 | async-start | bytes 163840
  9.7 18.0 %collective-permute-start = (f32[32,128]{0,1:T(8,128)S(1)}, f32[32,128]{0,1:T(8,128)S(1)}, u32[]{:S(2)}, u32[]{:S(2)}) collective-permute-start(f32[32,128]{0,1:T(8,128)S(1)} %bitcast.186), channel_id=1, source_target_pairs={{0,4},{4,8},{8,12},{12,16},{16,20},{20,24},{24,28},{28,32},{32,36}... | collective-permute-start | bytes 49160 | tf_op jit(solution)/shard_map/ppermute | solution.py:10
  15.4 12.4 %collective-permute-start.1 = (f32[32,128]{0,1:T(8,128)S(1)}, f32[32,128]{0,1:T(8,128)S(1)}, u32[]{:S(2)}, u32[]{:S(2)}) collective-permute-start(f32[32,128]{0,1:T(8,128)S(1)} %bitcast.183), channel_id=1, source_target_pairs={{4,0},{8,4},{12,8},{16,12},{20,16},{24,20},{28,24},{32,28},{36,32}... | collective-permute-start | bytes 49160 | tf_op jit(solution)/shard_map/ppermute | solution.py:10
  18.0 9.9 %collective-permute-start.2 = (f32[32,128]{0,1:T(8,128)S(1)}, f32[32,128]{0,1:T(8,128)S(1)}, u32[]{:S(2)}, u32[]{:S(2)}) collective-permute-start(f32[32,128]{0,1:T(8,128)S(1)} %bitcast.184), channel_id=1, source_target_pairs={{0,1},{1,2},{2,3},{4,5},{5,6},{6,7},{8,9},{9,10},{10,11},{12,13},{... | collective-permute-start | bytes 49160 | tf_op jit(solution)/shard_map/ppermute | solution.py:10
  20.5 7.5 collective-permute-start.3
  26.7 215.1 %copy-start.2 = (f32[1,1,80,1024]{3,2,1,0:T(8,128)S(1)}, f32[1,1,80,1024]{3,2,1,0:T(8,128)}, u32[]{:S(2)}) copy-start(f32[1,1,80,1024]{3,2,1,0:T(8,128)} %param.14) | copy-start | bytes 983044
  171.7 614.8 %reduce-scatter.9.cloned.1.call-start = ((), (), s32[]{:S(2)}) async-start(), calls=%async_computation.3 | async-start | bytes 163840
  228.2 18.9 %collective-permute-start.7 = (f32[32,128]{1,0:T(8,128)S(1)}, f32[32,128]{1,0:T(8,128)S(1)}, u32[]{:S(2)}, u32[]{:S(2)}) collective-permute-start(f32[32,128]{1,0:T(8,128)S(1)} %get-tuple-element.28), channel_id=1, source_target_pairs={{0,1},{1,2},{2,3},{4,5},{5,6},{6,7},{8,9},{9,10},{10,11},{12,13},{... | collective-permute-start | bytes 49160 | tf_op jit(solution)/shard_map/ppermute | solution.py:10
  230.1 16.9 %collective-permute-start.6 = (f32[32,128]{1,0:T(8,128)S(1)}, f32[32,128]{1,0:T(8,128)S(1)}, u32[]{:S(2)}, u32[]{:S(2)}) collective-permute-start(f32[32,128]{1,0:T(8,128)S(1)} %get-tuple-element.29), channel_id=1, source_target_pairs={{1,0},{2,1},{3,2},{5,4},{6,5},{7,6},{9,8},{10,9},{11,10},{13,12},{... | collective-permute-start | bytes 49160 | tf_op jit(solution)/shard_map/ppermute | solution.py:10
  235.2 11.6 %collective-permute-start.5 = (f32[32,128]{1,0:T(8,128)S(1)}, f32[32,128]{1,0:T(8,128)S(1)}, u32[]{:S(2)}, u32[]{:S(2)}) collective-permute-start(f32[32,128]{1,0:T(8,128)S(1)} %get-tuple-element.30), channel_id=1, source_target_pairs={{0,4},{4,8},{8,12},{12,16},{16,20},{20,24},{24,28},{28,32},{32,36}... | collective-permute-start | bytes 49160 | tf_op jit(solution)/shard_map/ppermute | solution.py:10
  239.9 6.8 collective-permute-start.4
  253.3 15.1 %collective-permute-start.8 = (f32[32,128]{0,1:T(8,128)S(1)}, f32[32,128]{0,1:T(8,128)S(1)}, u32[]{:S(2)}, u32[]{:S(2)}) collective-permute-start(f32[32,128]{0,1:T(8,128)S(1)} %bitcast.191), channel_id=1, source_target_pairs={{0,4},{4,8},{8,12},{12,16},{16,20},{20,24},{24,28},{28,32},{32,36}... | collective-permute-start | bytes 49160 | tf_op jit(solution)/shard_map/ppermute | solution.py:10
  257.2 11.2 %collective-permute-start.9 = (f32[32,128]{0,1:T(8,128)S(1)}, f32[32,128]{0,1:T(8,128)S(1)}, u32[]{:S(2)}, u32[]{:S(2)}) collective-permute-start(f32[32,128]{0,1:T(8,128)S(1)} %bitcast.193), channel_id=1, source_target_pairs={{4,0},{8,4},{12,8},{16,12},{20,16},{24,20},{28,24},{32,28},{36,32}... | collective-permute-start | bytes 49160 | tf_op jit(solution)/shard_map/ppermute | solution.py:10
  261.1 7.3 collective-permute-start.10
  263.1 7.0 collective-permute-start.11
  542.0 11.1 %copy-start.1 = (f32[16384,32]{1,0:T(8,128)S(1)}, f32[16384,32]{1,0:T(8,128)}, u32[]{:S(2)}) copy-start(f32[16384,32]{1,0:T(8,128)} %gather_fusion.10) | copy-start | bytes 6291460
  547.6 8.0 slice-start.2
  553.1 2.5 slice-start.3
  553.1 5.1 slice-start
  555.6 2.5 slice-start.1
  555.6 5.0 copy-start.4
  561.0 13.7 %collective-permute-start.12 = (f32[32,128]{0,1:T(8,128)S(1)}, f32[32,128]{0,1:T(8,128)S(1)}, u32[]{:S(2)}, u32[]{:S(2)}) collective-permute-start(f32[32,128]{0,1:T(8,128)S(1)} %get-tuple-element.13), channel_id=1, source_target_pairs={{4,0},{8,4},{12,8},{16,12},{20,16},{24,20},{28,24},{32,28},{36,32}... | collective-permute-start | bytes 49160 | tf_op jit(solution)/shard_map/ppermute | solution.py:10
  562.9 13.1 %collective-permute-start.13 = (f32[32,128]{0,1:T(8,128)S(1)}, f32[32,128]{0,1:T(8,128)S(1)}, u32[]{:S(2)}, u32[]{:S(2)}) collective-permute-start(f32[32,128]{0,1:T(8,128)S(1)} %get-tuple-element.12), channel_id=1, source_target_pairs={{0,4},{4,8},{8,12},{12,16},{16,20},{20,24},{24,28},{28,32},{32,36}... | collective-permute-start | bytes 49160 | tf_op jit(solution)/shard_map/ppermute | solution.py:10
  568.0 9.4 %collective-permute-start.14 = (f32[32,128]{0,1:T(8,128)S(1)}, f32[32,128]{0,1:T(8,128)S(1)}, u32[]{:S(2)}, u32[]{:S(2)}) collective-permute-start(f32[32,128]{0,1:T(8,128)S(1)} %get-tuple-element.11), channel_id=1, source_target_pairs={{1,0},{2,1},{3,2},{5,4},{6,5},{7,6},{9,8},{10,9},{11,10},{13,12},{... | collective-permute-start | bytes 49160 | tf_op jit(solution)/shard_map/ppermute | solution.py:10
  572.7 7.1 collective-permute-start.15
  583.8 228.4 %copy-start.3 = (f32[32,512]{1,0:T(8,128)}, f32[32,512]{1,0:T(8,128)S(1)}, u32[]{:S(2)}) copy-start(f32[32,512]{1,0:T(8,128)S(1)} %copy.111) | copy-start | bytes 196612
  583.9 13.0 %collective-permute-start.16 = (f32[32,128]{0,1:T(8,128)S(1)}, f32[32,128]{0,1:T(8,128)S(1)}, u32[]{:S(2)}, u32[]{:S(2)}) collective-permute-start(f32[32,128]{0,1:T(8,128)S(1)} %bitcast.192), channel_id=1, source_target_pairs={{0,4},{4,8},{8,12},{12,16},{16,20},{20,24},{24,28},{28,32},{32,36}... | collective-permute-start | bytes 49160 | tf_op jit(solution)/shard_map/ppermute | solution.py:10
  586.1 10.8 %collective-permute-start.17 = (f32[32,128]{0,1:T(8,128)S(1)}, f32[32,128]{0,1:T(8,128)S(1)}, u32[]{:S(2)}, u32[]{:S(2)}) collective-permute-start(f32[32,128]{0,1:T(8,128)S(1)} %bitcast.189), channel_id=1, source_target_pairs={{4,0},{8,4},{12,8},{16,12},{20,16},{24,20},{28,24},{32,28},{36,32}... | collective-permute-start | bytes 49160 | tf_op jit(solution)/shard_map/ppermute | solution.py:10
  589.7 7.3 collective-permute-start.18
  591.6 7.0 collective-permute-start.19
  793.6 18.9 %collective-permute-start.23 = (f32[32,128]{1,0:T(8,128)S(1)}, f32[32,128]{1,0:T(8,128)S(1)}, u32[]{:S(2)}, u32[]{:S(2)}) collective-permute-start(f32[32,128]{1,0:T(8,128)S(1)} %get-tuple-element.24), channel_id=1, source_target_pairs={{0,1},{1,2},{2,3},{4,5},{5,6},{6,7},{8,9},{9,10},{10,11},{12,13},{... | collective-permute-start | bytes 49160 | tf_op jit(solution)/shard_map/ppermute | solution.py:10
  795.5 16.9 %collective-permute-start.22 = (f32[32,128]{1,0:T(8,128)S(1)}, f32[32,128]{1,0:T(8,128)S(1)}, u32[]{:S(2)}, u32[]{:S(2)}) collective-permute-start(f32[32,128]{1,0:T(8,128)S(1)} %get-tuple-element.25), channel_id=1, source_target_pairs={{1,0},{2,1},{3,2},{5,4},{6,5},{7,6},{9,8},{10,9},{11,10},{13,12},{... | collective-permute-start | bytes 49160 | tf_op jit(solution)/shard_map/ppermute | solution.py:10
  800.6 11.6 %collective-permute-start.21 = (f32[32,128]{1,0:T(8,128)S(1)}, f32[32,128]{1,0:T(8,128)S(1)}, u32[]{:S(2)}, u32[]{:S(2)}) collective-permute-start(f32[32,128]{1,0:T(8,128)S(1)} %get-tuple-element.26), channel_id=1, source_target_pairs={{0,4},{4,8},{8,12},{12,16},{16,20},{20,24},{24,28},{28,32},{32,36}... | collective-permute-start | bytes 49160 | tf_op jit(solution)/shard_map/ppermute | solution.py:10
  805.3 6.8 collective-permute-start.20
Sparse Core Ops, SparseCore 0:
  171.8 49.2 reduce-scatter.6
  738.8 47.5 reduce-scatter.8
where the time goes:
time: 827 us; the launch traced here: 826 us
  local copies, waits for them, and re-layouts  286 us (35%)
  blocking collectives  269 us (33%)
  waiting for transfers between devices  111 us (13%)
  starting transfers between devices  81 us (10%)
  other arithmetic  37.1 us (4%)
  matrix products  26.4 us (3%)
  between operations  15 us (2%)
    gather x5, local copies, waits for them, and re-layouts, couple(): nearby = sub[:, index[begin:finish]]  272 us
    all_gather x2, blocking collectives, coarse_apply(): lax.all_gather(restricted, 'rows', axis=1, tiled=True)  269 us
    unnamed x4, waiting for transfers between devices  96.9 us
    ppermute x24, starting transfers between devices, from_behind(): return lax.ppermute(block, axis, route)  80.9 us
    reduce_sum x5, other arithmetic, couple(): coupled = coupled + jnp.sum(nearby * coef[None, begin:finish, :], axis=1)  18.5 us
  transfers between devices with their start and end apart: 26, of which 7 were waited for; matrix products, arithmetic and copies ran while one was open for 1% of the time, Pallas kernels for 0%

commit v1 on v0

--- a/solution.py
+++ b/solution.py
@@ -2,6 +2,13 @@
 import jax.numpy as jnp
 from jax import lax
 from jax.sharding import PartitionSpec as P
+
+
+def manage_surface_in(block_in, a_name):
+    f_next = lax.all_to_all(
+        jnp.stack([block_in] * lax.axis_size(a_name)), axis_name=a_name, split_axis=0, concat_axis=0
+    )
+    return jnp.concatenate(f_next, axis=1)
 
 
 def from_behind(block, axis, distance):
@@ -46,7 +53,7 @@
 def coarse_apply(restricted, coarse_block):
     highest = lax.Precision.HIGHEST
     partial_sum = lax.dot_general(
-        lax.all_gather(restricted, "rows", axis=1, tiled=True),
+        manage_surface_in(restricted, "rows"),
         coarse_block,
         (((1,), (1,)), ((), ())),
         precision=highest,

time: 827 us -> 574 us (0.69)
  blocking collectives: 269 us -> 22.3 us
  waiting for transfers between devices: 111 us -> 82.2 us
  starting transfers between devices: 81 us -> 92.5 us
    all_gather x2 -> x0, blocking collectives: 269 us -> none  [coarse_apply(): lax.all_gather(restricted, 'rows', axis=1, tiled=True)]
    unnamed x4, waiting for transfers between devices: 96.9 us -> 57 us
    all_to_all x0 -> x1, blocking collectives: none -> 22.3 us  [manage_surface_in(): lax.all_to_all(jnp.stack([block_in] * lax.axis_size(a_name)), axis_name=a...]
    all_to_all x0 -> x1, waiting for transfers between devices: none -> 12.1 us  [manage_surface_in(): lax.all_to_all(jnp.stack([block_in] * lax.axis_size(a_name)), axis_name=a...]
    all_to_all x0 -> x1, starting transfers between devices: none -> 11.7 us  [manage_surface_in(): lax.all_to_all(jnp.stack([block_in] * lax.axis_size(a_name)), axis_name=a...]
  transfers between devices with their start and end apart: 26 -> 27, of which waited for: 7 -> 8; matrix products, arithmetic and copies ran while one was open for 1% -> 2% of each run, Pallas kernels for 0% -> 0%
where the time goes in v1:
time: 574 us; the launch traced here: 573 us
  local copies, waits for them, and re-layouts  292 us (51%)
  starting transfers between devices  92.5 us (16%)
  waiting for transfers between devices  82.2 us (14%)
  other arithmetic  42.2 us (7%)
  matrix products  26.5 us (5%)
  blocking collectives  22.3 us (4%)
  between operations  15.1 us (3%)
    gather x5, local copies, waits for them, and re-layouts, couple(): nearby = sub[:, index[begin:finish]]  272 us
    ppermute x24, starting transfers between devices, from_behind(): return lax.ppermute(block, axis, route)  80.7 us
    unnamed x4, waiting for transfers between devices  57 us
    all_to_all x1, blocking collectives, manage_surface_in(): lax.all_to_all(jnp.stack([block_in] * lax.axis_size(a_name)), axis_name=a...  22.3 us
    reduce_sum x5, other arithmetic, couple(): coupled = coupled + jnp.sum(nearby * coef[None, begin:finish, :], axis=1)  18.5 us
    scatter-add x12, other arithmetic, fold(): owned = owned.at[:, sends[e]].add(backs[e])  16.6 us
    ppermute x24, waiting for transfers between devices, from_behind(): return lax.ppermute(block, axis, route)  13.1 us
    all_to_all x1, waiting for transfers between devices, manage_surface_in(): lax.all_to_all(jnp.stack([block_in] * lax.axis_size(a_name)), axis_name=a...  12.1 us
  transfers between devices with their start and end apart: 27, of which 8 were waited for; matrix products, arithmetic and copies ran while one was open for 2% of the time, Pallas kernels for 0%

profile of v1, /device:TPU:120, one launch (start us, length us, event | category | flops | bytes accessed | tf_op | source)
XLA Modules:
  0.0 572.5 jit_solution(10815104249092816097)
XLA Ops:
  9.7 5.0 collective-permute-start
  15.3 1.9 collective-permute-start.1
  18.0 1.9 collective-permute-start.2
  20.5 5.1 collective-permute-start.3
  29.9 11.7 %all-to-all-start = ((f32[64,1,2048]{2,1,0:T(1,128)}), f32[64,1,2048]{2,1,0:T(1,128)S(1)}, u32[]{:S(2)}, u32[]{:S(2)}) async-start(f32[64,1,2048]{2,1,0:T(1,128)} %reshape.554), calls=%async_computation | async-start | bytes 1048576 | tf_op jit(solution)/shard_map/all_to_all | solution.py:8
  43.0 12.1 %all-to-all-done = f32[64,1,2048]{2,1,0:T(1,128)S(1)} async-done(((f32[64,1,2048]{2,1,0:T(1,128)}), f32[64,1,2048]{2,1,0:T(1,128)S(1)}, u32[]{:S(2)}, u32[]{:S(2)}) %all-to-all-start) | async-done | bytes 524320 | tf_op jit(solution)/shard_map/all_to_all | solution.py:8
  55.7 1.9 reduce.10
  59.0 5.8 %convolution_bitcast_fusion.1 = f32[256,32]{1,0:T(8,128)} fusion(f32[32,4096]{1,0:T(8,128)S(1)} %reshape.302, f32[256,4096]{1,0:T(8,128)} %param.11), kind=kOutput, calls=%fused_computation.41 | convolution fusion | flops 402653184 | bytes 4751360
  64.9 28.4 %reduce-scatter.7.cloned.1.call-done = f32[64,32]{1,0:T(8,128)} async-done(((f32[256,32]{1,0:T(8,128)}), f32[64,32]{1,0:T(8,128)}) %reduce-scatter.7.cloned.1.call-update) | async-done | bytes 8208
  94.3 6.0 %fusion.4 = f32[32,1024]{1,0:T(8,128)S(1)} fusion(f32[32,1024]{1,0:T(8,128)S(1)} %fusion.14, f32[32,1024]{1,0:T(8,128)S(1)} %constant_dynamic-update-slice_fusion, f32[1,1,1024,1024]{3,2,1,0:T(8,128)} %param.9), kind=kOutput, calls=%fused_computation.38 | convolution fusion | flops 402685952 | bytes 4587520 | tf_op jit(solution)/shard_map/dot_general | solution.py:91
  100.4 1.9 collective-permute-start.7
  102.3 5.1 collective-permute-start.6
  107.5 4.7 collective-permute-start.5
  112.1 1.9 collective-permute-start.4
  115.2 3.8 collective-permute-done.4
  125.8 1.9 collective-permute-start.8
  130.1 3.9 collective-permute-start.9
  134.0 1.9 collective-permute-start.10
  135.9 5.1 collective-permute-start.11
  141.2 1.8 collective-permute-done.11
  143.0 54.4 %gather_fusion.12 = f32[16384,32]{1,0:T(8,128)} fusion(f32[32,1024]{0,1:T(8,128)S(1)} %constant_dynamic-update-slice_fusion.5, s32[16384]{0:T(1024)S(1)} %copy-done.3), kind=kCustom, calls=%fused_computation.12 | custom fusion | bytes 4259840 | tf_op jit(solution)/shard_map/gather | solution.py:71
  197.4 54.4 %gather_fusion.11 = f32[16384,32]{1,0:T(8,128)} fusion(f32[32,1024]{0,1:T(8,128)S(1)} %constant_dynamic-update-slice_fusion.5, s32[16384]{0:T(1024)S(1)} %broadcast_clamp_fusion.1), kind=kCustom, calls=%fused_computation.11 | custom fusion | bytes 4259840 | tf_op jit(solution)/shard_map/gather | solution.py:71
  251.8 54.4 %gather_fusion.10 = f32[16384,32]{1,0:T(8,128)} fusion(f32[32,1024]{0,1:T(8,128)S(1)} %constant_dynamic-update-slice_fusion.5, s32[16384]{0:T(1024)S(1)} %broadcast_clamp_fusion.2), kind=kCustom, calls=%fused_computation.10 | custom fusion | bytes 4259840 | tf_op jit(solution)/shard_map/gather | solution.py:71
  306.2 54.4 %gather_fusion.9 = f32[16384,32]{1,0:T(8,128)} fusion(f32[32,1024]{0,1:T(8,128)S(1)} %constant_dynamic-update-slice_fusion.5, s32[16384]{0:T(1024)S(1)} %copy-done.2), kind=kCustom, calls=%fused_computation.9 | custom fusion | bytes 4259840 | tf_op jit(solution)/shard_map/gather | solution.py:71
  360.6 54.3 %gather_fusion.8 = f32[16384,32]{1,0:T(8,128)} fusion(f32[32,1024]{0,1:T(8,128)S(1)} %constant_dynamic-update-slice_fusion.5, s32[16384]{0:T(1024)S(1)} %broadcast_clamp_fusion.4), kind=kCustom, calls=%fused_computation.8 | custom fusion | bytes 4259840 | tf_op jit(solution)/shard_map/gather | solution.py:71
  414.9 5.6 multiply_reduce_fusion
  420.5 5.4 multiply_reduce_fusion.1
  426.0 2.5 multiply_reduce_fusion.2
  428.5 2.5 multiply_reduce_fusion.3
  431.1 2.5 multiply_reduce_fusion.4
  433.8 1.9 collective-permute-start.12
  435.8 5.1 collective-permute-start.13
  440.9 4.6 collective-permute-start.14
  445.6 1.9 collective-permute-start.15
  457.2 2.2 collective-permute-start.16
  459.4 3.6 collective-permute-start.17
  463.1 1.9 collective-permute-start.18
  465.0 5.1 collective-permute-start.19
  473.3 22.3 %all_to_all.10 = f32[64,1,2048]{2,1,0:T(1,128)S(1)} all-to-all(f32[64,1,2048]{2,1,0:T(1,128)S(1)} %reshape.556), channel_id=1, replica_groups=mesh['rows'=64,'cols'=4] {'rows'}, dimensions={0} | all-to-all | bytes 1048576 | tf_op jit(solution)/shard_map/all_to_all | solution.py:8
  495.5 1.9 reduce.11
  498.8 5.8 %convolution_bitcast_fusion = f32[256,32]{1,0:T(8,128)} fusion(f32[32,4096]{1,0:T(8,128)S(1)} %reshape.304, f32[256,4096]{1,0:T(8,128)} %param.11), kind=kOutput, calls=%fused_computation.40 | convolution fusion | flops 402653184 | bytes 4751360
  504.7 28.6 %reduce-scatter.9.cloned.1.call-done = f32[64,32]{1,0:T(8,128)} async-done(((f32[256,32]{1,0:T(8,128)}), f32[64,32]{1,0:T(8,128)}) %reduce-scatter.9.cloned.1.call-update) | async-done | bytes 8208
  534.4 6.0 %fusion.7 = f32[32,1024]{1,0:T(8,128)S(1)} fusion(f32[32,1024]{1,0:T(8,128)S(1)} %fusion.10, f32[32,1024]{1,0:T(8,128)S(1)} %constant_dynamic-update-slice_fusion.10, f32[1,1,1024,1024]{3,2,1,0:T(8,128)} %param.9), kind=kOutput, calls=%fused_computation.39 | convolution fusion | flops 402685952 | bytes 4587520 | tf_op jit(solution)/shard_map/dot_general | solution.py:91
  540.4 1.9 collective-permute-start.23
  542.4 5.1 collective-permute-start.22
  547.5 4.7 collective-permute-start.21
  552.2 1.9 collective-permute-start.20
  554.3 4.8 collective-permute-done.20
  (154 shorter events, 45.6 us)
Async XLA Ops:
  7.2 20.8 %copy-start = (f32[1,1,64,1024]{3,2,1,0:T(8,128)S(1)}, f32[1,1,64,1024]{3,2,1,0:T(8,128)}, u32[]{:S(2)}) copy-start(f32[1,1,64,1024]{3,2,1,0:T(8,128)} %param.10) | copy-start | bytes 786436
  9.0 11.5 %copy-start.5 = (s32[1024]{0:T(1024)}, s32[1024]{0:T(1024)S(1)}, u32[]{:S(2)}) copy-start(s32[1024]{0:T(1024)S(1)} %get-tuple-element.39) | copy-start | bytes 12292
  9.0 17.7 %copy-start.6 = (s32[1024]{0:T(1024)}, s32[1024]{0:T(1024)S(1)}, u32[]{:S(2)}) copy-start(s32[1024]{0:T(1024)S(1)} %get-tuple-element.38) | copy-start | bytes 12292
  9.7 18.0 %collective-permute-start = (f32[32,128]{0,1:T(8,128)S(1)}, f32[32,128]{0,1:T(8,128)S(1)}, u32[]{:S(2)}, u32[]{:S(2)}) collective-permute-start(f32[32,128]{0,1:T(8,128)S(1)} %bitcast.179), channel_id=1, source_target_pairs={{0,4},{4,8},{8,12},{12,16},{16,20},{20,24},{24,28},{28,32},{32,36}... | collective-permute-start | bytes 49160 | tf_op jit(solution)/shard_map/ppermute | solution.py:17
  15.3 12.4 %collective-permute-start.1 = (f32[32,128]{0,1:T(8,128)S(1)}, f32[32,128]{0,1:T(8,128)S(1)}, u32[]{:S(2)}, u32[]{:S(2)}) collective-permute-start(f32[32,128]{0,1:T(8,128)S(1)} %bitcast.177), channel_id=1, source_target_pairs={{4,0},{8,4},{12,8},{16,12},{20,16},{24,20},{28,24},{32,28},{36,32}... | collective-permute-start | bytes 49160 | tf_op jit(solution)/shard_map/ppermute | solution.py:17
  17.3 0.7 copy-start.7
  17.3 9.4 %copy-start.8 = (s32[1024]{0:T(1024)}, s32[1024]{0:T(1024)S(1)}, u32[]{:S(2)}) copy-start(s32[1024]{0:T(1024)S(1)} %get-tuple-element.36) | copy-start | bytes 12292
  18.0 9.8 %collective-permute-start.2 = (f32[32,128]{0,1:T(8,128)S(1)}, f32[32,128]{0,1:T(8,128)S(1)}, u32[]{:S(2)}, u32[]{:S(2)}) collective-permute-start(f32[32,128]{0,1:T(8,128)S(1)} %bitcast.178), channel_id=1, source_target_pairs={{0,1},{1,2},{2,3},{4,5},{5,6},{6,7},{8,9},{9,10},{10,11},{12,13},{... | collective-permute-start | bytes 49160 | tf_op jit(solution)/shard_map/ppermute | solution.py:17
  20.5 7.3 %collective-permute-start.3 = (f32[32,128]{0,1:T(8,128)S(1)}, f32[32,128]{0,1:T(8,128)S(1)}, u32[]{:S(2)}, u32[]{:S(2)}) collective-permute-start(f32[32,128]{0,1:T(8,128)S(1)} %bitcast.175), channel_id=1, source_target_pairs={{1,0},{2,1},{3,2},{5,4},{6,5},{7,6},{9,8},{10,9},{11,10},{13,12},{... | collective-permute-start | bytes 49160 | tf_op jit(solution)/shard_map/ppermute | solution.py:17
  29.9 25.2 %all-to-all-start = ((f32[64,1,2048]{2,1,0:T(1,128)}), f32[64,1,2048]{2,1,0:T(1,128)S(1)}, u32[]{:S(2)}, u32[]{:S(2)}) async-start(f32[64,1,2048]{2,1,0:T(1,128)} %reshape.554), calls=%async_computation | async-start | bytes 1048576 | tf_op jit(solution)/shard_map/all_to_all | solution.py:8
  41.6 51.7 %reduce-scatter.7.cloned.1.call-start = ((), (), s32[]{:S(2)}) async-start(), calls=%async_computation.4 | async-start | bytes 163840
  58.6 84.4 %copy-start.3 = (s32[16384]{0:T(1024)S(1)}, s32[16384]{0:T(1024)}, u32[]{:S(2)}) copy-start(s32[16384]{0:T(1024)} %broadcast_clamp_fusion) | copy-start | bytes 196612
  64.8 468.5 %reduce-scatter.9.cloned.1.call-start = ((), (), s32[]{:S(2)}) async-start(), calls=%async_computation.5 | async-start | bytes 163840
  100.4 18.9 %collective-permute-start.7 = (f32[32,128]{1,0:T(8,128)S(1)}, f32[32,128]{1,0:T(8,128)S(1)}, u32[]{:S(2)}, u32[]{:S(2)}) collective-permute-start(f32[32,128]{1,0:T(8,128)S(1)} %get-tuple-element.28), channel_id=1, source_target_pairs={{0,1},{1,2},{2,3},{4,5},{5,6},{6,7},{8,9},{9,10},{10,11},{12,13},{... | collective-permute-start | bytes 49160 | tf_op jit(solution)/shard_map/ppermute | solution.py:17
  102.3 16.9 %collective-permute-start.6 = (f32[32,128]{1,0:T(8,128)S(1)}, f32[32,128]{1,0:T(8,128)S(1)}, u32[]{:S(2)}, u32[]{:S(2)}) collective-permute-start(f32[32,128]{1,0:T(8,128)S(1)} %get-tuple-element.29), channel_id=1, source_target_pairs={{1,0},{2,1},{3,2},{5,4},{6,5},{7,6},{9,8},{10,9},{11,10},{13,12},{... | collective-permute-start | bytes 49160 | tf_op jit(solution)/shard_map/ppermute | solution.py:17
  107.5 11.6 %collective-permute-start.5 = (f32[32,128]{1,0:T(8,128)S(1)}, f32[32,128]{1,0:T(8,128)S(1)}, u32[]{:S(2)}, u32[]{:S(2)}) collective-permute-start(f32[32,128]{1,0:T(8,128)S(1)} %get-tuple-element.30), channel_id=1, source_target_pairs={{0,4},{4,8},{8,12},{12,16},{16,20},{20,24},{24,28},{28,32},{32,36}... | collective-permute-start | bytes 49160 | tf_op jit(solution)/shard_map/ppermute | solution.py:17
  112.1 6.8 %collective-permute-start.4 = (f32[32,128]{1,0:T(8,128)S(1)}, f32[32,128]{1,0:T(8,128)S(1)}, u32[]{:S(2)}, u32[]{:S(2)}) collective-permute-start(f32[32,128]{1,0:T(8,128)S(1)} %get-tuple-element.31), channel_id=1, source_target_pairs={{4,0},{8,4},{12,8},{16,12},{20,16},{24,20},{28,24},{32,28},{36,32}... | collective-permute-start | bytes 49160 | tf_op jit(solution)/shard_map/ppermute | solution.py:17
  125.8 15.3 %collective-permute-start.8 = (f32[32,128]{0,1:T(8,128)S(1)}, f32[32,128]{0,1:T(8,128)S(1)}, u32[]{:S(2)}, u32[]{:S(2)}) collective-permute-start(f32[32,128]{0,1:T(8,128)S(1)} %bitcast.183), channel_id=1, source_target_pairs={{0,4},{4,8},{8,12},{12,16},{16,20},{20,24},{24,28},{28,32},{32,36}... | collective-permute-start | bytes 49160 | tf_op jit(solution)/shard_map/ppermute | solution.py:17
  130.1 11.0 %collective-permute-start.9 = (f32[32,128]{0,1:T(8,128)S(1)}, f32[32,128]{0,1:T(8,128)S(1)}, u32[]{:S(2)}, u32[]{:S(2)}) collective-permute-start(f32[32,128]{0,1:T(8,128)S(1)} %bitcast.185), channel_id=1, source_target_pairs={{4,0},{8,4},{12,8},{16,12},{20,16},{24,20},{28,24},{32,28},{36,32}... | collective-permute-start | bytes 49160 | tf_op jit(solution)/shard_map/ppermute | solution.py:17
  134.0 7.1 %collective-permute-start.10 = (f32[32,128]{0,1:T(8,128)S(1)}, f32[32,128]{0,1:T(8,128)S(1)}, u32[]{:S(2)}, u32[]{:S(2)}) collective-permute-start(f32[32,128]{0,1:T(8,128)S(1)} %bitcast.182), channel_id=1, source_target_pairs={{0,1},{1,2},{2,3},{4,5},{5,6},{6,7},{8,9},{9,10},{10,11},{12,13},{... | collective-permute-start | bytes 49160 | tf_op jit(solution)/shard_map/ppermute | solution.py:17
  135.9 7.0 %collective-permute-start.11 = (f32[32,128]{0,1:T(8,128)S(1)}, f32[32,128]{0,1:T(8,128)S(1)}, u32[]{:S(2)}, u32[]{:S(2)}) collective-permute-start(f32[32,128]{0,1:T(8,128)S(1)} %bitcast.180), channel_id=1, source_target_pairs={{1,0},{2,1},{3,2},{5,4},{6,5},{7,6},{9,8},{10,9},{11,10},{13,12},{... | collective-permute-start | bytes 49160 | tf_op jit(solution)/shard_map/ppermute | solution.py:17
  251.8 54.4 %copy-start.2 = (s32[16384]{0:T(1024)S(1)}, s32[16384]{0:T(1024)}, u32[]{:S(2)}) copy-start(s32[16384]{0:T(1024)} %broadcast_clamp_fusion.3) | copy-start | bytes 196612
  414.9 11.1 %copy-start.1 = (f32[16384,32]{1,0:T(8,128)S(1)}, f32[16384,32]{1,0:T(8,128)}, u32[]{:S(2)}) copy-start(f32[16384,32]{1,0:T(8,128)} %gather_fusion.10) | copy-start | bytes 6291460
  420.5 8.0 %slice-start.2 = ((s8[8388608]{0:T(1024)(128)(4,1)}), s8[4194304]{0:T(1024)(128)(4,1)S(1)}, s32[]{:S(2)}) async-start(s8[8388608]{0:T(1024)(128)(4,1)} %bitcast.153), calls=%async_computation.8 | async-start | bytes 8388608
  426.0 2.5 slice-start.3
  426.0 5.1 slice-start
  428.5 2.5 slice-start.1
  428.5 5.0 copy-start.9
  433.8 13.7 %collective-permute-start.12 = (f32[32,128]{0,1:T(8,128)S(1)}, f32[32,128]{0,1:T(8,128)S(1)}, u32[]{:S(2)}, u32[]{:S(2)}) collective-permute-start(f32[32,128]{0,1:T(8,128)S(1)} %get-tuple-element.13), channel_id=1, source_target_pairs={{4,0},{8,4},{12,8},{16,12},{20,16},{24,20},{28,24},{32,28},{36,32}... | collective-permute-start | bytes 49160 | tf_op jit(solution)/shard_map/ppermute | solution.py:17
  435.8 13.1 %collective-permute-start.13 = (f32[32,128]{0,1:T(8,128)S(1)}, f32[32,128]{0,1:T(8,128)S(1)}, u32[]{:S(2)}, u32[]{:S(2)}) collective-permute-start(f32[32,128]{0,1:T(8,128)S(1)} %get-tuple-element.12), channel_id=1, source_target_pairs={{0,4},{4,8},{8,12},{12,16},{16,20},{20,24},{24,28},{28,32},{32,36}... | collective-permute-start | bytes 49160 | tf_op jit(solution)/shard_map/ppermute | solution.py:17
  440.9 9.4 %collective-permute-start.14 = (f32[32,128]{0,1:T(8,128)S(1)}, f32[32,128]{0,1:T(8,128)S(1)}, u32[]{:S(2)}, u32[]{:S(2)}) collective-permute-start(f32[32,128]{0,1:T(8,128)S(1)} %get-tuple-element.11), channel_id=1, source_target_pairs={{1,0},{2,1},{3,2},{5,4},{6,5},{7,6},{9,8},{10,9},{11,10},{13,12},{... | collective-permute-start | bytes 49160 | tf_op jit(solution)/shard_map/ppermute | solution.py:17
  445.6 7.1 %collective-permute-start.15 = (f32[32,128]{0,1:T(8,128)S(1)}, f32[32,128]{0,1:T(8,128)S(1)}, u32[]{:S(2)}, u32[]{:S(2)}) collective-permute-start(f32[32,128]{0,1:T(8,128)S(1)} %get-tuple-element.10), channel_id=1, source_target_pairs={{0,1},{1,2},{2,3},{4,5},{5,6},{6,7},{8,9},{9,10},{10,11},{12,13},{... | collective-permute-start | bytes 49160 | tf_op jit(solution)/shard_map/ppermute | solution.py:17
  457.2 83.2 %copy-start.4 = (f32[32,512]{1,0:T(8,128)}, f32[32,512]{1,0:T(8,128)S(1)}, u32[]{:S(2)}) copy-start(f32[32,512]{1,0:T(8,128)S(1)} %copy.109) | copy-start | bytes 196612
  457.2 13.0 %collective-permute-start.16 = (f32[32,128]{0,1:T(8,128)S(1)}, f32[32,128]{0,1:T(8,128)S(1)}, u32[]{:S(2)}, u32[]{:S(2)}) collective-permute-start(f32[32,128]{0,1:T(8,128)S(1)} %bitcast.184), channel_id=1, source_target_pairs={{0,4},{4,8},{8,12},{12,16},{16,20},{20,24},{24,28},{28,32},{32,36}... | collective-permute-start | bytes 49160 | tf_op jit(solution)/shard_map/ppermute | solution.py:17
  459.4 10.8 %collective-permute-start.17 = (f32[32,128]{0,1:T(8,128)S(1)}, f32[32,128]{0,1:T(8,128)S(1)}, u32[]{:S(2)}, u32[]{:S(2)}) collective-permute-start(f32[32,128]{0,1:T(8,128)S(1)} %bitcast.181), channel_id=1, source_target_pairs={{4,0},{8,4},{12,8},{16,12},{20,16},{24,20},{28,24},{32,28},{36,32}... | collective-permute-start | bytes 49160 | tf_op jit(solution)/shard_map/ppermute | solution.py:17
  463.1 7.3 %collective-permute-start.18 = (f32[32,128]{0,1:T(8,128)S(1)}, f32[32,128]{0,1:T(8,128)S(1)}, u32[]{:S(2)}, u32[]{:S(2)}) collective-permute-start(f32[32,128]{0,1:T(8,128)S(1)} %bitcast.176), channel_id=1, source_target_pairs={{0,1},{1,2},{2,3},{4,5},{5,6},{6,7},{8,9},{9,10},{10,11},{12,13},{... | collective-permute-start | bytes 49160 | tf_op jit(solution)/shard_map/ppermute | solution.py:17
  465.0 7.0 %collective-permute-start.19 = (f32[32,128]{0,1:T(8,128)S(1)}, f32[32,128]{0,1:T(8,128)S(1)}, u32[]{:S(2)}, u32[]{:S(2)}) collective-permute-start(f32[32,128]{0,1:T(8,128)S(1)} %bitcast.174), channel_id=1, source_target_pairs={{1,0},{2,1},{3,2},{5,4},{6,5},{7,6},{9,8},{10,9},{11,10},{13,12},{... | collective-permute-start | bytes 49160 | tf_op jit(solution)/shard_map/ppermute | solution.py:17
  540.4 18.9 %collective-permute-start.23 = (f32[32,128]{1,0:T(8,128)S(1)}, f32[32,128]{1,0:T(8,128)S(1)}, u32[]{:S(2)}, u32[]{:S(2)}) collective-permute-start(f32[32,128]{1,0:T(8,128)S(1)} %get-tuple-element.24), channel_id=1, source_target_pairs={{0,1},{1,2},{2,3},{4,5},{5,6},{6,7},{8,9},{9,10},{10,11},{12,13},{... | collective-permute-start | bytes 49160 | tf_op jit(solution)/shard_map/ppermute | solution.py:17
  542.4 16.9 %collective-permute-start.22 = (f32[32,128]{1,0:T(8,128)S(1)}, f32[32,128]{1,0:T(8,128)S(1)}, u32[]{:S(2)}, u32[]{:S(2)}) collective-permute-start(f32[32,128]{1,0:T(8,128)S(1)} %get-tuple-element.25), channel_id=1, source_target_pairs={{1,0},{2,1},{3,2},{5,4},{6,5},{7,6},{9,8},{10,9},{11,10},{13,12},{... | collective-permute-start | bytes 49160 | tf_op jit(solution)/shard_map/ppermute | solution.py:17
  547.5 11.6 %collective-permute-start.21 = (f32[32,128]{1,0:T(8,128)S(1)}, f32[32,128]{1,0:T(8,128)S(1)}, u32[]{:S(2)}, u32[]{:S(2)}) collective-permute-start(f32[32,128]{1,0:T(8,128)S(1)} %get-tuple-element.26), channel_id=1, source_target_pairs={{0,4},{4,8},{8,12},{12,16},{16,20},{20,24},{24,28},{28,32},{32,36}... | collective-permute-start | bytes 49160 | tf_op jit(solution)/shard_map/ppermute | solution.py:17
  552.2 6.8 %collective-permute-start.20 = (f32[32,128]{1,0:T(8,128)S(1)}, f32[32,128]{1,0:T(8,128)S(1)}, u32[]{:S(2)}, u32[]{:S(2)}) collective-permute-start(f32[32,128]{1,0:T(8,128)S(1)} %get-tuple-element.27), channel_id=1, source_target_pairs={{4,0},{8,4},{12,8},{16,12},{20,16},{24,20},{28,24},{32,28},{36,32}... | collective-permute-start | bytes 49160 | tf_op jit(solution)/shard_map/ppermute | solution.py:17
Sparse Core Ops, SparseCore 0:
  64.9 28.2 reduce-scatter.6
  504.7 28.5 reduce-scatter.8
